TPU v7x, 128 devices: a whole 4x4x4 slice. The times are simulated.
128 devices in a mesh: section: 32 (over z, y, core), tensor: 4 (over x).
Axes of the slice: x: 4, y: 4, z: 4, core: 2. Of those that a mesh axis runs over, the one named last changes fastest.
Arguments:
- flight_state: bfloat16 [32, 512, 3584], P('section', 'tensor'), may hold values from -6 to 6
- flight_tokens: int32 [32, 3], P('section'), may hold values from 1 to 256, as said below
- flight_lists: int32 [32, 3], P('section'), may hold values from 0 to 1023, as said below
- incoming: bfloat16 [2, 512, 3584], P(None, 'tensor'), may hold values from -6 to 6
- incoming_tokens: int32 [2, 3], replicated, may hold values from 1 to 256, as said below
- norm_gain: float32 [32, 3584], P('section'), may hold values from 0.25 to 1.75
- query_weight: bfloat16 [32, 3584, 3584], P('section', None, 'tensor'), may hold values from -0.09375 to 0.09375
- query_bias: float32 [32, 3584], P('section', 'tensor'), may hold values from -10 to 10
- key_weight: bfloat16 [32, 3584, 512], P('section', None, 'tensor'), may hold values from -0.09375 to 0.09375
- key_bias: float32 [32, 512], P('section', 'tensor'), may hold values from -10 to 10
- value_weight: bfloat16 [32, 3584, 512], P('section', None, 'tensor'), may hold values from -0.09375 to 0.09375
- value_bias: float32 [32, 512], P('section', 'tensor'), may hold values from -3 to 3
- output_weight: bfloat16 [32, 3584, 3584], P('section', 'tensor'), may hold values from -0.09375 to 0.09375
- list_rows: int32 [1024], replicated, may hold values from 0 to 1023, each once
Outputs:
- next_state: bfloat16 [32, 512, 3584], P('section', 'tensor')
- list_sums: float32 [1024, 3584], P(('section', 'tensor'))
Inputs may be any that keep to these rules, and one draw needn't show every extreme that they name: `flight_tokens`: in each micro-batch the blocks ceil(tokens / 128) of its 3 programs sum to 4; in every draw some program has the most and some program has 1 token. `incoming_tokens`: in each micro-batch the blocks ceil(tokens / 128) of its 3 programs sum to 4; in every draw some program has the most and some program has 1 token. `flight_lists`: every micro-batch after the first gives one of its programs the list of some program of the micro-batch before it.
All inputs are finite; a program needn't handle non-finite values.
Results may differ from a plain program's by a relative error of at most 0.034.
Values may be sent and summed in bfloat16 or wider, within the bound.
A program may use at most 128 MiB of HBM per device.

v0:
```python
import math

import jax
import jax.numpy as jnp
from jax import lax
from jax.sharding import PartitionSpec as P

HEAD = 128
LAYERS = 28
BLOCK = 128


EPS = 1e-06
THETA = 1000000.0


def from_behind(block, axis, distance):
    devices = range(lax.axis_size(axis))
    route = [((i - distance) % len(devices), i) for i in devices]
    return lax.ppermute(block, axis, route)


def broadcast(value, axis, root):
    mine = lax.axis_index(axis) == root
    return lax.psum(jnp.where(mine, value, jnp.zeros_like(value)), axis)


def as_sent(value):
    return jax.tree.map(lambda a: a.astype(jnp.bfloat16) if a.dtype == jnp.float32 else a, value)


def row_layout(tokens, first, count):
    blocks = (tokens + BLOCK - 1) // BLOCK
    ends = (jnp.cumsum(blocks) * BLOCK).astype(jnp.int32)
    starts = ends - blocks * BLOCK
    slots = first + jnp.arange(count, dtype=jnp.int32)
    program = jnp.sum((slots[:, None] >= ends[None, :]).astype(jnp.int32), axis=1)
    chosen = program[:, None] == jnp.arange(tokens.shape[0], dtype=jnp.int32)[None, :]
    begin = jnp.sum(jnp.where(chosen, starts[None, :], 0), axis=1)
    length = jnp.sum(jnp.where(chosen, tokens[None, :], 0), axis=1)
    position = slots - begin
    return (program, position, position < length)


def rotate(values, position):
    half = values.shape[-1] // 2
    freq = THETA ** (-jnp.arange(half, dtype=jnp.float32) * 2.0 / values.shape[-1])
    angle = position.astype(jnp.float32)[:, None] * freq[None, :]
    cosine = jnp.cos(angle)[:, None, :]
    sine = jnp.sin(angle)[:, None, :]
    first_half = values[..., :half]
    second_half = values[..., half:]
    return jnp.concatenate(
        [first_half * cosine - second_half * sine, second_half * cosine + first_half * sine],
        axis=-1,
    )


def attend(queries, key_rows, value_rows, program, valid):
    total = queries.shape[0]
    width = min(512, total)
    scale = 1.0 / math.sqrt(queries.shape[-1])

    def one_block(index):
        scores = (
            jnp.einsum("qcgd,kcd->cgqk", queries, key_rows, preferred_element_type=jnp.float32)
            * scale
        )
        allowed = (program[:, None] == program[None, :]) & valid[None, :]
        scores = jnp.where(allowed[None, None], scores, -1e30)
        top = jnp.max(scores, axis=-1, keepdims=True)
        expo = jnp.exp(scores - top)
        probs = (expo / jnp.sum(expo, axis=-1, keepdims=True)).astype(jnp.bfloat16)
        mixed = jnp.einsum("cgqk,kcd->qcgd", probs, value_rows, preferred_element_type=jnp.float32)
        return mixed.astype(jnp.bfloat16)

    blocks = lax.map(one_block, jnp.arange(total // width, dtype=jnp.int32))
    return blocks.reshape(total, -1)


def normalize(state, gain):
    values = state.astype(jnp.float32)
    return (
        values * lax.rsqrt(jnp.mean(values * values, axis=-1, keepdims=True) + EPS) * gain
    ).astype(jnp.bfloat16)


def local(
    flight_state,
    flight_tokens,
    flight_lists,
    incoming,
    incoming_tokens,
    norm_gain,
    query_weight,
    query_bias,
    key_weight,
    key_bias,
    value_weight,
    value_bias,
    output_weight,
    list_rows,
):
    tensor_count = lax.axis_size("tensor")
    section_count = lax.axis_size("section")
    tensor_rank = lax.axis_index("tensor")
    section_rank = lax.axis_index("section")
    is_last = section_rank == section_count - 1
    active = section_rank < min(section_count, LAYERS)
    own_rows = flight_state.shape[1]
    all_rows = own_rows * tensor_count
    row_first = tensor_rank * own_rows
    query_cols = query_weight.shape[2]
    key_cols = key_weight.shape[2]
    kv_local = key_cols // HEAD
    groups = query_cols // key_cols
    gain = norm_gain[0]
    prog_count = flight_tokens.shape[1]

    def assemble(rows):
        return lax.all_gather(rows, "tensor", axis=0, tiled=True)

    tokens = flight_tokens[0]
    lists = flight_lists[0]
    part_list = []
    token_list = []
    lists_list = []
    whole = assemble(flight_state[0])
    for tick in range(incoming.shape[0]):
        piece = normalize(whole, gain)
        combined = jnp.concatenate(
            [
                jnp.dot(piece, query_weight[0], preferred_element_type=jnp.float32),
                jnp.dot(piece, key_weight[0], preferred_element_type=jnp.float32),
                jnp.dot(piece, value_weight[0], preferred_element_type=jnp.float32),
            ],
            axis=1,
        )
        heads_program, heads_position, heads_valid = row_layout(tokens, 0, all_rows)
        query_f = combined[:, :query_cols] + query_bias[0]
        key_f = combined[:, query_cols : query_cols + key_cols] + key_bias[0]
        value_f = combined[:, query_cols + key_cols :] + value_bias[0]
        queries = rotate(query_f.reshape(all_rows, kv_local * groups, HEAD), heads_position).astype(
            jnp.bfloat16
        )
        queries = queries.reshape(all_rows, kv_local, groups, HEAD)
        key_rows = rotate(key_f.reshape(all_rows, kv_local, HEAD), heads_position).astype(
            jnp.bfloat16
        )
        value_rows = value_f.astype(jnp.bfloat16).reshape(all_rows, kv_local, HEAD)
        mixed = attend(queries, key_rows, value_rows, heads_program, heads_valid)
        rows_now = lax.dynamic_slice_in_dim(whole, row_first, own_rows, 0)
        summed = lax.psum_scatter(
            jnp.dot(mixed, output_weight[0], preferred_element_type=jnp.float32).astype(
                jnp.bfloat16
            ),
            "tensor",
            scatter_dimension=0,
            tiled=True,
        ).astype(jnp.float32)
        mapped = (rows_now.astype(jnp.float32) + summed).astype(jnp.bfloat16)
        rows_out = jnp.where(active, mapped, rows_now)
        program, position, valid = row_layout(tokens, row_first, own_rows)
        member = (
            (program[None, :] == jnp.arange(prog_count, dtype=jnp.int32)[:, None]) & valid[None, :]
        ).astype(jnp.bfloat16)
        part_list.append(jnp.dot(member, rows_out, preferred_element_type=jnp.float32))
        token_list.append(tokens)
        lists_list.append(lists)
        outgoing = jnp.where(is_last, incoming[tick], rows_out)
        sent_tokens = jnp.where(is_last, incoming_tokens[tick], tokens)
        sent_lists = jnp.where(is_last, jnp.zeros_like(lists), lists)
        whole, tokens, lists = from_behind(
            (assemble(outgoing), sent_tokens, sent_lists), "section", 1
        )
    state_rows = lax.dynamic_slice_in_dim(whole, row_first, own_rows, 0)
    parts = jnp.stack(part_list)
    counts = jnp.stack(token_list)
    exit_lists = jnp.stack(lists_list)
    total = lax.psum(parts.astype(jnp.bfloat16), "tensor").astype(jnp.float32)
    means = total / counts[..., None].astype(jnp.float32)
    embedded = means * lax.rsqrt(jnp.mean(means * means, axis=-1, keepdims=True) + EPS)
    embedded, exit_lists = (
        broadcast(embedded.astype(jnp.bfloat16), "section", section_count - 1).astype(
            embedded.dtype
        ),
        broadcast(as_sent(exit_lists), "section", section_count - 1).astype(exit_lists.dtype),
    )
    flat = embedded.reshape(-1, embedded.shape[-1])
    flat_lists = exit_lists.reshape(-1)
    list_total = list_rows.shape[0]
    target = jnp.sum(
        jnp.where(
            flat_lists[:, None] == jnp.arange(list_total, dtype=jnp.int32)[None, :],
            list_rows[None, :],
            0,
        ),
        axis=1,
    )
    local_count = list_total // (section_count * tensor_count)
    owned = lax.axis_index(("section", "tensor")) * local_count + jnp.arange(
        local_count, dtype=jnp.int32
    )
    select = (owned[:, None] == target[None, :]).astype(jnp.float32)
    list_sums = jnp.dot(select, flat, precision=lax.Precision.HIGHEST)
    return (state_rows[None], list_sums)


def solution(mesh):
    in_specs = (
        P("section", "tensor", None),
        P("section", None),
        P("section", None),
        P(None, "tensor", None),
        P(),
        P("section", None),
        P("section", None, "tensor"),
        P("section", "tensor"),
        P("section", None, "tensor"),
        P("section", "tensor"),
        P("section", None, "tensor"),
        P("section", "tensor"),
        P("section", "tensor", None),
        P(),
    )
    out_specs = (P("section", "tensor", None), P(("section", "tensor"), None))
    return jax.shard_map(local, mesh=mesh, in_specs=in_specs, out_specs=out_specs, check_vma=False)
```

profile of v0, /device:TPU:0, one launch (start us, length us, event | category | flops | bytes accessed | tf_op | source)
XLA Modules:
  0.0 579.1 jit_solution(16477160890725204429)
XLA Ops:
  12.8 3.1 collective-permute-done.1
  16.8 2.7 multiply_cosine_fusion
  19.5 36.6 %all-gather.9.cloned.1.call-done = bf16[1,512,3584]{2,1,0:T(8,128)(2,1)} async-done(((bf16[1,128,3584]{2,1,0:T(8,128)(2,1)}), bf16[1,512,3584]{2,1,0:T(8,128)(2,1)}) %all-gather.9.cloned.1.call-update) | async-done | bytes 3670032 | tf_op jit(solution)/shard_map/all_gather | solution.py:121
  56.1 3.0 fusion.3
  62.0 5.3 fusion.32
  72.5 3.0 copy.56
  82.6 7.6 %fusion.38 = bf16[128,7,512]{2,0,1:T(8,128)(2,1)S(1)} fusion(f32[7,512]{1,0:T(8,128)S(1)} %fusion.6, f32[7,512]{1,0:T(8,128)S(1)} %get-tuple-element.72, f32[512,512,7]{1,0,2:T(8,128)} %copy-done.2, pred[512,512]{0,1:T(8,128)(4,1)S(1)} %compare_and_fusion.1, bf16[1,3584,128]{2,1,0:T(8,128)(2,1)S(1)} %copy-done, f32[128]{0:T(128)S(1)} %bitcast.180, ...), kind=kOutput, calls=%fused_computation.48 | convolution fusion | flops 956628992 | bytes 13152768 | tf_op jit(solution)/shard_map/while/body/eval_jaxpr/cgqk,kcd->qcgd/dot_general | solution.py:74
  90.2 8.3 %fusion.16 = bf16[512,3584]{1,0:T(8,128)(2,1)} fusion(bf16[512,896]{0,1:T(8,128)(2,1)S(1)} %bitcast.183, bf16[1,896,3584]{2,1,0:T(8,128)(2,1)} %param.26), kind=kOutput, calls=%fused_computation.26 | convolution fusion | flops 3290169344 | bytes 11010048 | tf_op jit(solution)/shard_map/dot_general | solution.py:154
  98.6 42.9 %reduce-scatter.3.cloned.1.call-done = bf16[128,3584]{1,0:T(8,128)(2,1)} async-done(((bf16[512,3584]{1,0:T(8,128)(2,1)}), bf16[128,3584]{1,0:T(8,128)(2,1)}) %reduce-scatter.3.cloned.1.call-update) | async-done | bytes 917520 | tf_op jit(solution)/shard_map/reduce_scatter | solution.py:153
  141.5 2.8 bitcast_select_fusion.2
  144.3 43.7 %all-gather.5.cloned.1.call-done = bf16[512,3584]{1,0:T(8,128)(2,1)} async-done(((bf16[128,3584]{1,0:T(8,128)(2,1)}), bf16[512,3584]{1,0:T(8,128)(2,1)}) %all-gather.5.cloned.1.call-update) | async-done | bytes 3670032 | tf_op jit(solution)/shard_map/all_gather | solution.py:121
  188.5 45.6 %collective-permute-done = bf16[512,3584]{1,0:T(8,128)(2,1)S(1)} collective-permute-done((bf16[512,3584]{1,0:T(8,128)(2,1)}, bf16[512,3584]{1,0:T(8,128)(2,1)S(1)}, u32[]{:S(2)}, u32[]{:S(2)}) %collective-permute-start) | collective-permute-done | bytes 3670048 | tf_op jit(solution)/shard_map/ppermute | solution.py:20
  238.4 8.1 %fusion.35 = f32[512,896]{1,0:T(8,128)} fusion(bf16[1,3584,896]{2,1,0:T(8,128)(2,1)} %param.20, f32[896]{0:T(1024)S(1)} %copy-done.22, bf16[512,3584]{1,0:T(8,128)(2,1)S(1)} %collective-permute-done, f32[512]{0:T(512)S(1)} %add_rsqrt_fusion, f32[3584]{0:T(1024)S(1)} %copy-done.13), kind=kOutput, calls=%fused_computation.47 | convolution fusion | flops 3296133120 | bytes 11947520 | tf_op jit(solution)/shard_map/dot_general | solution.py:133
  251.5 3.0 copy.58
  258.6 3.0 copy-done.1
  263.1 7.6 %fusion.41 = bf16[128,7,512]{2,0,1:T(8,128)(2,1)S(1)} fusion(f32[7,512]{1,0:T(8,128)S(1)} %fusion.7, f32[7,512]{1,0:T(8,128)S(1)} %get-tuple-element.74, f32[512,512,7]{1,0,2:T(8,128)} %copy-done.1, pred[512,512]{0,1:T(8,128)(4,1)S(1)} %compare_and_fusion, bf16[1,3584,128]{2,1,0:T(8,128)(2,1)S(1)} %copy-done, f32[128]{0:T(128)S(1)} %bitcast.181, ...), kind=kOutput, calls=%fused_computation.49 | convolution fusion | flops 956628992 | bytes 13152768 | tf_op jit(solution)/shard_map/while/body/eval_jaxpr/cgqk,kcd->qcgd/dot_general | solution.py:74
  270.7 8.3 %fusion.19 = bf16[512,3584]{1,0:T(8,128)(2,1)} fusion(bf16[512,896]{0,1:T(8,128)(2,1)S(1)} %bitcast.182, bf16[1,896,3584]{2,1,0:T(8,128)(2,1)} %param.26), kind=kOutput, calls=%fused_computation.27 | convolution fusion | flops 3290169344 | bytes 11010048 | tf_op jit(solution)/shard_map/dot_general | solution.py:154
  279.1 39.6 %reduce-scatter.5.cloned.1.call-done = bf16[128,3584]{1,0:T(8,128)(2,1)} async-done(((bf16[512,3584]{1,0:T(8,128)(2,1)}), bf16[128,3584]{1,0:T(8,128)(2,1)}) %reduce-scatter.5.cloned.1.call-update) | async-done | bytes 917520 | tf_op jit(solution)/shard_map/reduce_scatter | solution.py:153
  318.7 2.8 bitcast_select_fusion.3
  321.5 43.8 %all-gather.7.cloned.1.call-done = bf16[512,3584]{1,0:T(8,128)(2,1)} async-done(((bf16[128,3584]{1,0:T(8,128)(2,1)}), bf16[512,3584]{1,0:T(8,128)(2,1)}) %all-gather.7.cloned.1.call-update) | async-done | bytes 3670032 | tf_op jit(solution)/shard_map/all_gather | solution.py:121
  366.9 44.3 %collective-permute-done.3 = s32[3]{0:T(128)S(1)} collective-permute-done((s32[3]{0:T(128)S(1)}, s32[3]{0:T(128)S(1)}, u32[]{:S(2)}, u32[]{:S(2)}) %collective-permute-start.3) | collective-permute-done | bytes 44 | tf_op jit(solution)/shard_map/ppermute | solution.py:20
  411.3 13.5 %psum.21 = s32[6]{0:T(128)S(1)} all-reduce(s32[6]{0:T(128)S(1)} %eq.173), channel_id=1, replica_groups=mesh['section'=32,'tensor'=4] {'section'}, use_global_device_ids=true, to_apply=%region_16.17 | all-reduce | flops 6 | bytes 48 | tf_op jit(solution)/shard_map/psum | solution.py:25
  429.1 15.9 %psum.22 = bf16[2,3,3584]{2,1,0:T(4,128)(2,1)S(1)} all-reduce(bf16[2,3,3584]{2,1,0:T(4,128)(2,1)S(1)} %pad_maximum_fusion), channel_id=1, replica_groups=mesh['section'=32,'tensor'=4] {'tensor'}, use_global_device_ids=true, to_apply=%region_24.25 | all-reduce | flops 21504 | bytes 86016 | tf_op jit(solution)/shard_map/psum | solution.py:180
  445.3 123.9 %psum.23 = bf16[6,3584]{1,0:T(8,128)(2,1)S(1)} all-reduce(bf16[6,3584]{1,0:T(8,128)(2,1)S(1)} %reshape.609), channel_id=1, replica_groups=mesh['section'=32,'tensor'=4] {'section'}, use_global_device_ids=true, to_apply=%region_26.27 | all-reduce | flops 21504 | bytes 86016 | tf_op jit(solution)/shard_map/psum | solution.py:25
  (155 shorter events, 46.5 us)
Async XLA Ops:
  7.2 75.5 %copy-start = (bf16[1,3584,128]{2,1,0:T(8,128)(2,1)S(1)}, bf16[1,3584,128]{2,1,0:T(8,128)(2,1)}, u32[]{:S(2)}) copy-start(bf16[1,3584,128]{2,1,0:T(8,128)(2,1)} %param.24) | copy-start | bytes 2752516
  7.2 51.9 %copy-start.35 = (bf16[1,3584,128]{2,1,0:T(8,128)(2,1)S(1)}, bf16[1,3584,128]{2,1,0:T(8,128)(2,1)}, u32[]{:S(2)}) copy-start(bf16[1,3584,128]{2,1,0:T(8,128)(2,1)} %param.22) | copy-start | bytes 2752516
  7.2 51.9 %copy-start.37 = (f32[1,128]{1,0:T(1,128)S(1)}, f32[1,128]{1,0:T(1,128)}, u32[]{:S(2)}) copy-start(f32[1,128]{1,0:T(1,128)} %param.23) | copy-start | bytes 1540
  7.2 48.9 %all-gather.9.cloned.1.call-start = ((), (), s32[]{:S(2)}) async-start(), calls=%async_computation.6 | async-start | bytes 4587520 | tf_op jit(solution)/shard_map/all_gather | solution.py:121
  7.9 133.5 %reduce-scatter.3.cloned.1.call-start = ((), (), s32[]{:S(2)}) async-start(), calls=%async_computation.2 | async-start | bytes 4587520 | tf_op jit(solution)/shard_map/reduce_scatter | solution.py:153
  8.7 7.2 %collective-permute-start.1 = (s32[3]{0:T(128)S(1)}, s32[3]{0:T(128)S(1)}, u32[]{:S(2)}, u32[]{:S(2)}) collective-permute-start(s32[3]{0:T(128)S(1)} %broadcast_select_fusion.1), channel_id=1, source_target_pairs={{124,0},{0,4},{4,8},{8,12},{12,16},{16,20},{20,24},{24,28},{28,32}... | collective-permute-start | bytes 44 | tf_op jit(solution)/shard_map/ppermute | solution.py:20
  9.4 52.5 %copy-start.21 = (f32[896]{0:T(1024)}, f32[896]{0:T(1024)S(1)}, u32[]{:S(2)}) copy-start(f32[896]{0:T(1024)S(1)} %reduce.5) | copy-start | bytes 10756
  10.1 51.8 %copy-start.11 = (f32[3584]{0:T(1024)}, f32[3584]{0:T(1024)S(1)}, u32[]{:S(2)}) copy-start(f32[3584]{0:T(1024)S(1)} %reduce.4) | copy-start | bytes 43012
  11.0 49.7 %copy-start.16 = (f32[64]{0:T(128)}, f32[64]{0:T(128)S(1)}, u32[]{:S(2)}) copy-start(f32[64]{0:T(128)S(1)} %multiply_power_fusion) | copy-start | bytes 772
  98.5 89.5 %all-gather.5.cloned.1.call-start = ((), (), s32[]{:S(2)}) async-start(), calls=%async_computation.3 | async-start | bytes 4587520 | tf_op jit(solution)/shard_map/all_gather | solution.py:121
  144.3 90.6 %copy-start.36 = (bf16[1,3584,128]{2,1,0:T(8,128)(2,1)S(1)}, bf16[1,3584,128]{2,1,0:T(8,128)(2,1)}, u32[]{:S(2)}) copy-start(bf16[1,3584,128]{2,1,0:T(8,128)(2,1)} %param.22) | copy-start | bytes 2752516
  144.3 174.4 %reduce-scatter.5.cloned.1.call-start = ((), (), s32[]{:S(2)}) async-start(), calls=%async_computation.4 | async-start | bytes 4587520 | tf_op jit(solution)/shard_map/reduce_scatter | solution.py:153
  188.1 46.0 %collective-permute-start = (bf16[512,3584]{1,0:T(8,128)(2,1)}, bf16[512,3584]{1,0:T(8,128)(2,1)S(1)}, u32[]{:S(2)}, u32[]{:S(2)}) collective-permute-start(bf16[512,3584]{1,0:T(8,128)(2,1)} %all-gather.5.cloned.1.call-done), channel_id=1, source_target_pairs={{124,0},{0,4},{4,8},{8,12},{12,16},{16,20},{20,24},{24,28},{28,32}... | collective-permute-start | bytes 11010056 | tf_op jit(solution)/shard_map/ppermute | solution.py:20
  279.0 86.3 %copy-start.33 = (s32[1,3]{1,0:T(1,128)S(1)}, s32[1,3]{1,0:T(1,128)}, u32[]{:S(2)}) copy-start(s32[1,3]{1,0:T(1,128)} %param.16) | copy-start | bytes 40
  279.0 145.8 %copy-start.15 = (s32[1,3]{1,0:T(1,128)S(1)}, s32[1,3]{1,0:T(1,128)}, u32[]{:S(2)}) copy-start(s32[1,3]{1,0:T(1,128)} %param.15) | copy-start | bytes 40
  279.0 145.8 %copy-start.19 = (s32[3]{0:T(128)S(1)}, s32[3]{0:T(128)}, u32[]{:S(2)}) copy-start(s32[3]{0:T(128)} %copy-done.18) | copy-start | bytes 40
  279.0 145.8 %copy-start.20 = (s32[1024]{0:T(1024)S(1)}, s32[1024]{0:T(1024)}, u32[]{:S(2)}) copy-start(s32[1024]{0:T(1024)} %param.27) | copy-start | bytes 12292
  279.0 146.0 %copy-start.28 = (s32[3]{0:T(128)S(1)}, s32[3]{0:T(128)}, u32[]{:S(2)}) copy-start(s32[3]{0:T(128)} %copy-done.27) | copy-start | bytes 40
  279.0 146.0 %copy-start.30 = (s32[3]{0:T(128)S(1)}, s32[3]{0:T(128)}, u32[]{:S(2)}) copy-start(s32[3]{0:T(128)} %copy-done.29) | copy-start | bytes 40
  279.1 146.1 %copy-start.24 = (s32[3]{0:T(128)S(1)}, s32[3]{0:T(128)}, u32[]{:S(2)}) copy-start(s32[3]{0:T(128)} %copy-done.23) | copy-start | bytes 40
  279.1 146.2 %copy-start.26 = (s32[3]{0:T(128)S(1)}, s32[3]{0:T(128)}, u32[]{:S(2)}) copy-start(s32[3]{0:T(128)} %copy-done.25) | copy-start | bytes 40
  279.1 86.2 %all-gather.7.cloned.1.call-start = ((), (), s32[]{:S(2)}) async-start(), calls=%async_computation.5 | async-start | bytes 4587520 | tf_op jit(solution)/shard_map/all_gather | solution.py:121
  365.3 204.8 %collective-permute-start.2 = (bf16[512,3584]{1,0:T(8,128)(2,1)}, bf16[512,3584]{1,0:T(8,128)(2,1)}, u32[]{:S(2)}, u32[]{:S(2)}) collective-permute-start(bf16[512,3584]{1,0:T(8,128)(2,1)} %all-gather.7.cloned.1.call-done), channel_id=1, source_target_pairs={{124,0},{0,4},{4,8},{8,12},{12,16},{16,20},{20,24},{24,28},{28,32}... | collective-permute-start | bytes 11010056 | tf_op jit(solution)/shard_map/ppermute | solution.py:20
  365.3 45.9 %collective-permute-start.3 = (s32[3]{0:T(128)S(1)}, s32[3]{0:T(128)S(1)}, u32[]{:S(2)}, u32[]{:S(2)}) collective-permute-start(s32[3]{0:T(128)S(1)} %fusion.115), channel_id=1, source_target_pairs={{124,0},{0,4},{4,8},{8,12},{12,16},{16,20},{20,24},{24,28},{28,32}... | collective-permute-start | bytes 44 | tf_op jit(solution)/shard_map/ppermute | solution.py:20
  (25 other events, 137.6 us)
Sparse Core Ops, SparseCore 0:
  9.7 46.3 all-gather.8
  98.7 42.7 reduce-scatter.2
  144.4 43.6 all-gather.4
  279.2 39.4 reduce-scatter.4
  321.6 43.6 all-gather.6
where the time goes:
time: 586 us; the launch traced here: 579 us
  waiting for transfers between devices  300 us (51%)
  blocking collectives  153 us (26%)
  matrix products  57.4 us (10%)
  other arithmetic  27.9 us (5%)
  local copies, waits for them, and re-layouts  23.6 us (4%)
  between operations  14.7 us (3%)
    psum x2, blocking collectives, broadcast(): return lax.psum(jnp.where(mine, value, jnp.zeros_like(value)), axis)  137 us
    all_gather x3, waiting for transfers between devices, assemble(): return lax.all_gather(rows, 'tensor', axis=0, tiled=True)  124 us
    ppermute x4, waiting for transfers between devices, from_behind(): return lax.ppermute(block, axis, route)  93 us
    reduce_scatter x2, waiting for transfers between devices, local(): lax.psum_scatter(jnp.dot(mixed, output_weight[0], preferred_element_type=...  82.4 us
    dot_general x2, matrix products, local(): jnp.dot(mixed, output_weight[0], preferred_element_type=jnp.float32)  16.6 us
    psum x1, blocking collectives, local(): total = lax.psum(parts.astype(jnp.bfloat16), 'tensor').astype(jnp.float32)  15.9 us
    dot_general x2, matrix products, one_block(): jnp.einsum('cgqk,kcd->qcgd', probs, value_rows, preferred_element_type=jn...  15.2 us
    unnamed x84, local copies, waits for them, and re-layouts  14.6 us
  transfers between devices with their start and end apart: 9, of which 8 were waited for; matrix products, arithmetic and copies ran while one was open for 2% of the time, Pallas kernels for 0%

commit v1 on v0

v1 whole, which is shorter than its diff:
```python
import math

import jax
import jax.numpy as jnp
import numpy as np
from jax import lax
from jax.experimental import pallas as pl
from jax.experimental.pallas import tpu as pltpu
from jax.sharding import PartitionSpec as P

HEAD = 128
LAYERS = 28
BLOCK = 128
EPS = 1e-06
THETA = 1000000.0

NT = 4
NC = 4
CR = BLOCK // NC
HR = CR // 2
NEG = -1e30
MESH = pl.DeviceIdType.MESH


def rope_tables():
    half = HEAD // 2
    freq = THETA ** (-np.arange(half, dtype=np.float64) * 2.0 / HEAD)
    freq = freq.astype(np.float32).astype(np.float64)
    angle = np.arange(2 * BLOCK, dtype=np.float64)[:, None] * freq[None, :]
    cosine, sine = np.cos(angle), np.sin(angle)
    return (
        np.concatenate([cosine, cosine], 1).astype(np.float32),
        np.concatenate([-sine, sine], 1).astype(np.float32),
    )


def kernel(
    n_sections,
    n_layers,
    flight,
    tokens,
    lists,
    incoming,
    inc_tokens,
    gain,
    wq_hbm,
    qb,
    wk_hbm,
    kb,
    wv_hbm,
    vb,
    wo_hbm,
    list_rows,
    cos_tab,
    sin_tab,
    out,
    sums,
    w,
    wo,
    x,
    y,
    g,
    part,
    ra,
    rb,
    fl,
    fr,
    q_s,
    k_s,
    v_s,
    mixed,
    rc,
    rs,
    mask,
    tok,
    pool,
    pool_part,
    w_sem,
    x_sem,
    inc_sem,
    ag_s,
    ag_r,
    rs_s,
    rs_r,
    hop_s,
    hop_r,
    tok_s,
    tok_r,
    pp_s,
    pp_r,
    pb_s,
    pb_r,
):
    s = lax.axis_index("section")
    t = lax.axis_index("tensor")
    right, left, opp = lax.rem(t + 1, NT), lax.rem(t + 3, NT), lax.rem(t + 2, NT)
    nxt, prv = lax.rem(s + 1, n_sections), lax.rem(s + n_sections - 1, n_sections)
    last = n_sections - 1
    active = s < n_layers
    dim = gain.shape[1]
    qcols = qb.shape[1]
    heads = qcols // HEAD

    loads = [
        pltpu.make_async_copy(wk_hbm.at[0], w.at[:, pl.ds(0, HEAD)], w_sem.at[0]),
        pltpu.make_async_copy(wv_hbm.at[0], w.at[:, pl.ds(HEAD, HEAD)], w_sem.at[1]),
        pltpu.make_async_copy(wq_hbm.at[0], w.at[:, pl.ds(2 * HEAD, qcols)], w_sem.at[2]),
        pltpu.make_async_copy(wo_hbm.at[0], wo, w_sem.at[3]),
    ]

    def x_load(c):
        return pltpu.make_async_copy(
            flight.at[0, pl.ds(c * CR, CR)], x.at[0, c], x_sem.at[c]
        )

    def inc_load(c):
        return pltpu.make_async_copy(
            incoming.at[0, pl.ds(c * CR, CR)], x.at[1, c], inc_sem.at[c]
        )

    inc_out = pltpu.make_async_copy(incoming.at[1], out.at[0], inc_sem.at[NC])

    for c in range(NC):
        x_load(c).start()

    @pl.when(active)
    def _():
        for load in loads:
            load.start()

    @pl.when(s == 0)
    def _():
        for c in range(NC):
            inc_load(c).start()
        inc_out.start()

    bar = pltpu.get_barrier_semaphore()
    for peer in (left, right, opp):
        pl.semaphore_signal(bar, inc=1, device_id=(s, peer), device_id_type=MESH)
    pl.semaphore_signal(bar, inc=1, device_id=(prv, t), device_id_type=MESH)
    for root in (last - 1, last):

        @pl.when(s != root)
        def _():
            pl.semaphore_signal(bar, inc=1, device_id=(root, t), device_id_type=MESH)

    @pl.when(s < last - 1)
    def _():
        pl.semaphore_wait(bar, 4)

    @pl.when(s >= last - 1)
    def _():
        pl.semaphore_wait(bar, 4 + n_sections - 1)

    row8 = lax.broadcasted_iota(jnp.int32, (8, HEAD), 0)

    def token_rows(ref):
        return jnp.where(
            row8 == 0, ref[0, 0], jnp.where(row8 == 1, ref[0, 1], ref[0, 2])
        )

    tok[0] = token_rows(tokens)
    tok_copy = pltpu.make_async_remote_copy(
        tok.at[0], tok.at[1], tok_s, tok_r, device_id=(nxt, t), device_id_type=MESH
    )

    @pl.when(s != last)
    def _():
        tok_copy.start()

    @pl.when(s == 0)
    def _():
        tok[1] = token_rows(inc_tokens)

    def layout(k, b):
        n = [tok[k, p : p + 1, :] for p in range(3)]
        e0 = jnp.where(n[0] > BLOCK, 2, 1)
        e1 = e0 + jnp.where(n[1] > BLOCK, 2, 1)
        prog = jnp.where(b >= e0, 1, 0) + jnp.where(b >= e1, 1, 0)
        begin = jnp.where(prog == 0, 0, jnp.where(prog == 1, e0, e1))
        length = jnp.where(prog == 0, n[0], jnp.where(prog == 1, n[1], n[2]))
        return prog, b - begin, length

    def remote(src, dst, ssem, rsem, dev):
        return pltpu.make_async_remote_copy(
            src, dst, ssem, rsem, device_id=dev, device_id_type=MESH
        )

    def rows(ref, k, c, b, first=0, count=CR):
        return ref.at[k, c, pl.ds(pl.multiple_of(b * CR + first, HR), count)]

    def ag_send(k, c, kind):
        if kind == 0:
            r, dev = rows(g, k, c, t), (s, right)
        elif kind == 1:
            r, dev = rows(g, k, c, t), (s, left)
        elif kind == 2:
            r, dev = rows(g, k, c, left, 0, HR), (s, right)
        else:
            r, dev = rows(g, k, c, right, HR, HR), (s, left)
        return remote(r, r, ag_s.at[k, c, kind], ag_r.at[k, c, kind], dev)

    def ag_recv(k, c, kind):
        if kind == 0:
            r, dev = rows(g, k, c, left), (s, left)
        elif kind == 1:
            r, dev = rows(g, k, c, right), (s, right)
        elif kind == 2:
            r, dev = rows(g, k, c, opp, 0, HR), (s, left)
        else:
            r, dev = rows(g, k, c, opp, HR, HR), (s, right)
        return remote(r, r, ag_s.at[k, c, kind], ag_r.at[k, c, kind], dev)

    def rs_copy(k, c, kind):
        if kind == 0:
            src, dst, dev = rows(part, k, c, opp, 0, HR), ra.at[k, c], (s, left)
        elif kind == 1:
            src, dst, dev = rows(part, k, c, opp, HR, HR), rb.at[k, c], (s, right)
        elif kind == 2:
            src, dst, dev = rows(part, k, c, left, HR, HR), fr.at[k, c, pl.ds(HR, HR)], (s, left)
        elif kind == 3:
            src, dst, dev = rows(part, k, c, right, 0, HR), fl.at[k, c, pl.ds(0, HR)], (s, right)
        elif kind == 4:
            src, dst, dev = rows(part, k, c, left, 0, HR), fr.at[k, c, pl.ds(0, HR)], (s, left)
        else:
            src, dst, dev = rows(part, k, c, right, HR, HR), fl.at[k, c, pl.ds(HR, HR)], (s, right)
        return remote(src, dst, rs_s.at[k, c, kind], rs_r.at[k, c, kind], dev)

    def hop(k, c, src):
        if k == 0:
            dst = x.at[1, c]
        else:
            dst = out.at[0, pl.ds(pl.multiple_of(c * CR, CR), CR)]
        return remote(src, dst, hop_s.at[k, c], hop_r.at[k, c], (nxt, t))

    lane_row = lax.broadcasted_iota(jnp.int32, (8, HEAD), 1)

    def pool_bcast(slot, j):
        dev = (lax.rem(s + j, n_sections), t)
        return remote(pool.at[slot], pool.at[slot], pb_s.at[j], pb_r.at[slot], dev)

    def pool_parts(d):
        dev = (s, lax.rem(t + d, NT))
        return remote(pool_part.at[0], pool_part.at[d], pp_s.at[d - 1], pp_r.at[d - 1], dev)

    def pool_root(slot):
        prog, second, length = layout(0, t)
        member = (row8 == prog) & (lane_row + BLOCK * second < length)
        member = jnp.where(member, 1.0, 0.0).astype(jnp.bfloat16)
        whole = x[0].reshape(BLOCK, dim)
        pool_part[0] = jnp.dot(member, whole, preferred_element_type=jnp.float32)
        for d in range(1, NT):
            pool_parts(d).start()
        for d in range(1, NT):
            pool_parts(d).wait_recv()
        total = pool_part[0] + pool_part[1] + pool_part[2] + pool_part[3]
        count = tok[0][:, :1].astype(jnp.float32)
        mean = total / count
        emb = mean * lax.rsqrt(jnp.mean(mean * mean, axis=-1, keepdims=True) + EPS)
        pool[slot, :, 0:dim] = emb
        target = [list_rows[lists[0, p]] for p in range(3)]
        target = jnp.where(
            row8 == 0, target[0], jnp.where(row8 == 1, target[1], target[2])
        )
        target = jnp.where(row8 < 3, target, -1)
        pool[slot, :, dim : dim + HEAD] = target.astype(jnp.float32)

        def send(j, _):
            pool_bcast(slot, j).start()
            return 0

        lax.fori_loop(1, n_sections, send, 0)

    def setup(k):
        i = lax.broadcasted_iota(jnp.int32, (1, HEAD), 1)
        info = [layout(k, b) for b in range(NT)]
        for b in range(NT):
            for kb_ in range(NT):
                ok = (info[b][0] == info[kb_][0]) & (i + BLOCK * info[kb_][1] < info[kb_][2])
                mask[b : b + 1, kb_ * BLOCK : (kb_ + 1) * BLOCK] = jnp.where(ok, 0.0, NEG)
        for b in range(NT):
            second = info[b][1] > 0
            for c in range(NC):
                lo, hi = c * CR, (c + 1) * CR
                rc[c, b * CR : (b + 1) * CR] = jnp.where(
                    second, cos_tab[BLOCK + lo : BLOCK + hi], cos_tab[lo:hi]
                )
                rs[c, b * CR : (b + 1) * CR] = jnp.where(
                    second, sin_tab[BLOCK + lo : BLOCK + hi], sin_tab[lo:hi]
                )

    def ag_issue(k, c):
        v = x[k, c].astype(jnp.float32)
        scale = lax.rsqrt(jnp.mean(v * v, axis=-1, keepdims=True) + EPS)
        rows(g, k, c, t)[...] = (v * scale * gain[...]).astype(jnp.bfloat16)
        ag_send(k, c, 0).start()
        ag_send(k, c, 1).start()

    def forward(k, c):
        ag_recv(k, c, 0).wait_recv()
        ag_send(k, c, 2).start()
        ag_recv(k, c, 1).wait_recv()
        ag_send(k, c, 3).start()

    def wait_opp(k, c):
        ag_recv(k, c, 2).wait_recv()
        ag_recv(k, c, 3).wait_recv()

    def rope(v, c):
        return (v * rc[c] + pltpu.roll(v, HEAD // 2, 1) * rs[c]).astype(jnp.bfloat16)

    def qkv(k, c):
        lhs = g[k, c]
        kv = jnp.dot(lhs, w[:, 0 : 2 * HEAD], preferred_element_type=jnp.float32)
        key = rope(kv[:, :HEAD] + kb[...], c)
        val = (kv[:, HEAD:] + vb[...]).astype(jnp.bfloat16)
        for b in range(NT):
            at = pl.ds(pl.multiple_of(b * BLOCK + c * CR, CR), CR)
            k_s[at, :] = key[b * CR : (b + 1) * CR]
            v_s[at, :] = val[b * CR : (b + 1) * CR]
        for h0 in range(0, heads, 2):
            n = min(2, heads - h0)
            q = jnp.dot(
                lhs,
                w[:, (2 + h0) * HEAD : (2 + h0 + n) * HEAD],
                preferred_element_type=jnp.float32,
            )
            for j in range(n):
                h = h0 + j
                v = q[:, j * HEAD : (j + 1) * HEAD] + qb[:, h * HEAD : (h + 1) * HEAD]
                v = rope(v, c)
                for b in range(NT):
                    q_s[c, b, h * CR : (h + 1) * CR, :] = v[b * CR : (b + 1) * CR]

    def attention(c):
        scale = 1.0 / math.sqrt(HEAD)
        for b in range(NT):
            lo, hi = max(b - 1, 0) * BLOCK, min(b + 2, NT) * BLOCK
            sc = lax.dot_general(
                q_s[c, b],
                k_s[lo:hi, :],
                (((1,), (1,)), ((), ())),
                preferred_element_type=jnp.float32,
            )
            sc = sc * scale + mask[b : b + 1, lo:hi]
            e = jnp.exp(sc - jnp.max(sc, axis=-1, keepdims=True))
            p = (e * (1.0 / jnp.sum(e, axis=-1, keepdims=True))).astype(jnp.bfloat16)
            o = jnp.dot(p, v_s[lo:hi, :], preferred_element_type=jnp.float32)
            o = o.astype(jnp.bfloat16)
            for h in range(heads):
                mixed[b * CR : (b + 1) * CR, h * HEAD : (h + 1) * HEAD] = o[
                    h * CR : (h + 1) * CR
                ]

    def project(k, c):
        width = 512
        lhs = mixed[...]

        def tile(n, _):
            at = pl.ds(pl.multiple_of(n * width, width), width)
            part[k, c, :, at] = jnp.dot(
                lhs, wo[:, at], preferred_element_type=jnp.float32
            ).astype(jnp.bfloat16)
            return 0

        lax.fori_loop(0, dim // width, tile, 0)
        for kind in range(4):
            rs_copy(k, c, kind).start()

    def add_on(k, c):
        rs_copy(k, c, 0).wait_recv()
        r = rows(part, k, c, left, 0, HR)
        r[...] = (r[...].astype(jnp.float32) + ra[k, c].astype(jnp.float32)).astype(jnp.bfloat16)
        rs_copy(k, c, 4).start()
        rs_copy(k, c, 1).wait_recv()
        r = rows(part, k, c, right, HR, HR)
        r[...] = (r[...].astype(jnp.float32) + rb[k, c].astype(jnp.float32)).astype(jnp.bfloat16)
        rs_copy(k, c, 5).start()

    def finish(k, c):
        for kind in range(2, 6):
            rs_copy(k, c, kind).wait_recv()
        f32 = jnp.float32
        total = (
            rows(part, k, c, t)[...].astype(f32)
            + fl[k, c].astype(f32)
            + fr[k, c].astype(f32)
        )
        y[k, c] = (x[k, c].astype(f32) + total).astype(jnp.bfloat16)
        hop(k, c, y.at[k, c]).start()

    def wait_x1(c):
        @pl.when(s == 0)
        def _():
            inc_load(c).wait()

        @pl.when(s != 0)
        def _():
            hop(0, c, y.at[0, c]).wait_recv()

    def gather_phase(k, ahead):
        def step(c, _):
            forward(k, c)

            @pl.when(c + ahead < NC)
            def _():
                if k == 1:
                    wait_x1(c + ahead)
                ag_issue(k, c + ahead)

            @pl.when(c >= 1)
            def _():
                wait_opp(k, c - 1)
                qkv(k, c - 1)

            return 0

        lax.fori_loop(0, NC, step, 0)
        wait_opp(k, NC - 1)
        qkv(k, NC - 1)

    def reduce_phase(k):
        def step(c, _):
            attention(c)
            project(k, c)

            @pl.when(c >= 1)
            def _():
                add_on(k, c - 1)

            @pl.when(c >= 2)
            def _():
                finish(k, c - 2)

            return 0

        lax.fori_loop(0, NC, step, 0)
        add_on(k, NC - 1)
        if k == 0:
            wait_x1(0)
            ag_issue(1, 0)
        finish(k, NC - 2)
        if k == 0:
            wait_x1(1)
            ag_issue(1, 1)
        finish(k, NC - 1)

    def wait_tokens():
        @pl.when(s != 0)
        def _():
            tok_copy.wait_recv()

    @pl.when(active)
    def _():
        for c in range(2):
            x_load(c).wait()
            ag_issue(0, c)
        for c in range(2, NC):
            x_load(c).wait()
        setup(0)
        for load in loads[:3]:
            load.wait()
        gather_phase(0, 2)
        loads[3].wait()
        reduce_phase(0)
        wait_tokens()
        setup(1)
        gather_phase(1, 2)
        reduce_phase(1)

        def drain(i, _):
            c, k = lax.rem(i, NC), lax.div(i, NC)
            for kind in range(4):
                ag_send(k, c, kind).wait_send()
            for kind in range(6):
                rs_copy(k, c, kind).wait_send()
            return 0

        lax.fori_loop(0, 2 * NC, drain, 0)

    @pl.when(jnp.logical_not(active))
    def _():
        for c in range(NC):
            x_load(c).wait()

            @pl.when(s != last)
            def _():
                hop(0, c, x.at[0, c]).start()

        for slot, root in ((0, last), (1, last - 1)):

            @pl.when(s == root)
            def _():
                pool_root(slot)

        for c in range(NC):
            hop(0, c, x.at[0, c]).wait_recv()

            @pl.when(s != last)
            def _():
                hop(1, c, x.at[1, c]).start()

        wait_tokens()

        for slot, root in ((0, last), (1, last - 1)):

            @pl.when(s == root)
            def _():
                def done(j, _):
                    pool_bcast(slot, j).wait_send()
                    return 0

                lax.fori_loop(1, n_sections, done, 0)
                for d in range(1, NT):
                    pool_parts(d).wait_send()

    for slot, root in ((0, last), (1, last - 1)):

        @pl.when(s != root)
        def _():
            pool_bcast(slot, 0).wait_recv()

    own = sums.shape[0]
    mine = ((s * NT + t) * own + lax.broadcasted_iota(jnp.int32, (own, HEAD), 0)).astype(jnp.float32)
    total = jnp.zeros((own, dim), jnp.float32)
    for slot in range(2):
        for p in range(3):
            hit = mine == pool[slot, p : p + 1, dim : dim + HEAD]
            hit = jnp.where(hit, 1.0, 0.0)[:, :1]
            total = total + hit * pool[slot, p : p + 1, 0:dim]
    sums[...] = total

    @pl.when(s != last)
    def _():
        tok_copy.wait_send()
        for k in range(2):
            for c in range(NC):
                hop(k, c, y.at[k, c]).wait_send()

    @pl.when(s != 0)
    def _():
        for c in range(NC):
            hop(1, c, y.at[1, c]).wait_recv()

    @pl.when(s == 0)
    def _():
        inc_out.wait()


def solution(mesh):
    n_sections = mesh.shape["section"]
    n_layers = min(n_sections, LAYERS)
    cos_np, sin_np = rope_tables()

    def local(
        flight_state,
        flight_tokens,
        flight_lists,
        incoming,
        incoming_tokens,
        norm_gain,
        query_weight,
        query_bias,
        key_weight,
        key_bias,
        value_weight,
        value_bias,
        output_weight,
        list_rows,
    ):
        dim = flight_state.shape[-1]
        qcols = query_weight.shape[-1]
        heads = qcols // HEAD
        own = list_rows.shape[0] // (n_sections * NT)
        bf16, f32 = jnp.bfloat16, jnp.float32
        dma = pltpu.SemaphoreType.DMA
        hbm = pl.BlockSpec(memory_space=pl.ANY)
        vmem = pl.BlockSpec(memory_space=pltpu.VMEM)
        smem = pl.BlockSpec(memory_space=pltpu.SMEM)

        def body(*refs):
            kernel(n_sections, n_layers, *refs)

        return pl.pallas_call(
            body,
            out_shape=(
                jax.ShapeDtypeStruct(flight_state.shape, bf16),
                jax.ShapeDtypeStruct((own, dim), f32),
            ),
            in_specs=[
                hbm, smem, smem, hbm, smem, vmem, hbm, vmem, hbm, vmem, hbm, vmem, hbm, smem, vmem, vmem,
            ],
            out_specs=(hbm, vmem),
            scratch_shapes=[
                pltpu.VMEM((dim, qcols + 2 * HEAD), bf16),
                pltpu.VMEM((qcols, dim), bf16),
                pltpu.VMEM((2, NC, CR, dim), bf16),
                pltpu.VMEM((2, NC, CR, dim), bf16),
                pltpu.VMEM((2, NC, NT * CR, dim), bf16),
                pltpu.VMEM((2, NC, NT * CR, dim), bf16),
                pltpu.VMEM((2, NC, HR, dim), bf16),
                pltpu.VMEM((2, NC, HR, dim), bf16),
                pltpu.VMEM((2, NC, CR, dim), bf16),
                pltpu.VMEM((2, NC, CR, dim), bf16),
                pltpu.VMEM((NC, NT, heads * CR, HEAD), bf16),
                pltpu.VMEM((NT * BLOCK, HEAD), bf16),
                pltpu.VMEM((NT * BLOCK, HEAD), bf16),
                pltpu.VMEM((NT * CR, qcols), bf16),
                pltpu.VMEM((NC, NT * CR, HEAD), f32),
                pltpu.VMEM((NC, NT * CR, HEAD), f32),
                pltpu.VMEM((8, NT * BLOCK), f32),
                pltpu.VMEM((2, 8, HEAD), jnp.int32),
                pltpu.VMEM((2, 8, dim + HEAD), f32),
                pltpu.VMEM((NT, 8, dim), f32),
                dma((4,)),
                dma((NC,)),
                dma((NC + 1,)),
                dma((2, NC, 4)),
                dma((2, NC, 4)),
                dma((2, NC, 6)),
                dma((2, NC, 6)),
                dma((2, NC)),
                dma((2, NC)),
                dma,
                dma,
                dma((NT - 1,)),
                dma((NT - 1,)),
                dma((n_sections,)),
                dma((2,)),
            ],
            compiler_params=pltpu.CompilerParams(
                collective_id=0,
                has_side_effects=True,
                vmem_limit_bytes=60 * 1024 * 1024,
            ),
        )(
            flight_state,
            flight_tokens,
            flight_lists,
            incoming,
            incoming_tokens,
            norm_gain,
            query_weight,
            query_bias,
            key_weight,
            key_bias,
            value_weight,
            value_bias,
            output_weight,
            list_rows,
            jnp.asarray(cos_np),
            jnp.asarray(sin_np),
        )

    in_specs = (
        P("section", "tensor", None),
        P("section", None),
        P("section", None),
        P(None, "tensor", None),
        P(),
        P("section", None),
        P("section", None, "tensor"),
        P("section", "tensor"),
        P("section", None, "tensor"),
        P("section", "tensor"),
        P("section", None, "tensor"),
        P("section", "tensor"),
        P("section", "tensor", None),
        P(),
    )
    out_specs = (P("section", "tensor", None), P(("section", "tensor"), None))
    return jax.shard_map(local, mesh=mesh, in_specs=in_specs, out_specs=out_specs, check_vma=False)
```

time: 586 us -> 151 us (0.26)
  the two profiles are of different devices: /device:TPU:0 before, /device:TPU:32 now
where the time goes in v1:
time: 151 us
  Pallas kernels  146 us (97%)
  local copies, waits for them, and re-layouts  3.71 us (2%)
    pallas_call x1, Pallas kernels, local(): pl.pallas_call(body, out_shape=(jax.ShapeDtypeStruct(flight_state.shape,...  146 us
    unnamed x2, local copies, waits for them, and re-layouts  3.71 us

profile of v1, /device:TPU:32, one launch (start us, length us, event | category | flops | bytes accessed | tf_op | source)
XLA Modules:
  0.0 150.5 jit_solution(10853279898174451053)
XLA Ops:
  0.6 146.2 %shard_map.167 = (bf16[1,128,3584]{2,1,0:T(8,128)(2,1)}, f32[8,3584]{1,0:T(8,128)}) custom-call(bf16[1,128,3584]{2,1,0:T(8,128)(2,1)} %refs_0_.1, s32[1,3]{1,0:T(1,128)} %refs_1_.1, s32[1,3]{1,0:T(1,128)} %refs_2_.1, bf16[2,128,3584]{2,1,0:T(8,128)(2,1)} %refs_3_.1, s32[2,3]{1,0:T(2,128)} %refs_4_.1, f32[1,3584]{1,0:T(1,128)} %refs_5_.1, ...), custom_call_target="tpu_custom_call" | custom-call | tf_op jit(solution)/shard_map/pallas_call | solution.py:584
  146.8 2.2 %copy.20 = bf16[1,128,3584]{2,1,0:T(8,128)(2,1)} copy(bf16[1,128,3584]{2,1,0:T(8,128)(2,1)} %get-tuple-element.4) | data formatting | bytes 1835008
  149.0 1.6 %copy.21 = f32[8,3584]{1,0:T(8,128)} copy(f32[8,3584]{1,0:T(8,128)} %get-tuple-element.5) | data formatting | bytes 229376

commit v2 on v1

--- a/solution.py
+++ b/solution.py
@@ -101,6 +101,14 @@
     qcols = qb.shape[1]
     heads = qcols // HEAD
 
+    def rows(ref, k, c, b, first=0, count=CR):
+        return ref.at[k, c, pl.ds(pl.multiple_of(b * CR + first, HR), count)]
+
+    def norm(k, c):
+        v = x[k, c].astype(jnp.float32)
+        scale = lax.rsqrt(jnp.mean(v * v, axis=-1, keepdims=True) + EPS)
+        rows(g, k, c, t)[...] = (v * scale * gain[...]).astype(jnp.bfloat16)
+
     loads = [
         pltpu.make_async_copy(wk_hbm.at[0], w.at[:, pl.ds(0, HEAD)], w_sem.at[0]),
         pltpu.make_async_copy(wv_hbm.at[0], w.at[:, pl.ds(HEAD, HEAD)], w_sem.at[1]),
@@ -143,6 +151,14 @@
         @pl.when(s != root)
         def _():
             pl.semaphore_signal(bar, inc=1, device_id=(root, t), device_id_type=MESH)
+
+    for c in range(NC):
+        x_load(c).wait()
+
+    @pl.when(active)
+    def _():
+        for c in range(NC):
+            norm(0, c)
 
     @pl.when(s < last - 1)
     def _():
@@ -185,9 +201,6 @@
         return pltpu.make_async_remote_copy(
             src, dst, ssem, rsem, device_id=dev, device_id_type=MESH
         )
-
-    def rows(ref, k, c, b, first=0, count=CR):
-        return ref.at[k, c, pl.ds(pl.multiple_of(b * CR + first, HR), count)]
 
     def ag_send(k, c, kind):
         if kind == 0:
@@ -226,12 +239,13 @@
             src, dst, dev = rows(part, k, c, right, HR, HR), fl.at[k, c, pl.ds(HR, HR)], (s, right)
         return remote(src, dst, rs_s.at[k, c, kind], rs_r.at[k, c, kind], dev)
 
-    def hop(k, c, src):
+    def hop(k, c, half, src):
         if k == 0:
-            dst = x.at[1, c]
+            dst = x.at[1, c, pl.ds(half * HR, HR)]
         else:
-            dst = out.at[0, pl.ds(pl.multiple_of(c * CR, CR), CR)]
-        return remote(src, dst, hop_s.at[k, c], hop_r.at[k, c], (nxt, t))
+            dst = out.at[0, pl.ds(pl.multiple_of(c * CR + half * HR, HR), HR)]
+        src = src.at[k, c, pl.ds(half * HR, HR)]
+        return remote(src, dst, hop_s.at[k, c, half], hop_r.at[k, c, half], (nxt, t))
 
     lane_row = lax.broadcasted_iota(jnp.int32, (8, HEAD), 1)
 
@@ -289,10 +303,7 @@
                     second, sin_tab[BLOCK + lo : BLOCK + hi], sin_tab[lo:hi]
                 )
 
-    def ag_issue(k, c):
-        v = x[k, c].astype(jnp.float32)
-        scale = lax.rsqrt(jnp.mean(v * v, axis=-1, keepdims=True) + EPS)
-        rows(g, k, c, t)[...] = (v * scale * gain[...]).astype(jnp.bfloat16)
+    def ag_start(k, c):
         ag_send(k, c, 0).start()
         ag_send(k, c, 1).start()
 
@@ -309,15 +320,17 @@
     def rope(v, c):
         return (v * rc[c] + pltpu.roll(v, HEAD // 2, 1) * rs[c]).astype(jnp.bfloat16)
 
-    def qkv(k, c):
-        lhs = g[k, c]
-        kv = jnp.dot(lhs, w[:, 0 : 2 * HEAD], preferred_element_type=jnp.float32)
+    def keys_values(k, c):
+        kv = jnp.dot(g[k, c], w[:, 0 : 2 * HEAD], preferred_element_type=jnp.float32)
         key = rope(kv[:, :HEAD] + kb[...], c)
         val = (kv[:, HEAD:] + vb[...]).astype(jnp.bfloat16)
         for b in range(NT):
             at = pl.ds(pl.multiple_of(b * BLOCK + c * CR, CR), CR)
             k_s[at, :] = key[b * CR : (b + 1) * CR]
             v_s[at, :] = val[b * CR : (b + 1) * CR]
+
+    def queries(k, c):
+        lhs = g[k, c]
         for h0 in range(0, heads, 2):
             n = min(2, heads - h0)
             q = jnp.dot(
@@ -334,36 +347,36 @@
 
     def attention(c):
         scale = 1.0 / math.sqrt(HEAD)
-        for b in range(NT):
-            lo, hi = max(b - 1, 0) * BLOCK, min(b + 2, NT) * BLOCK
-            sc = lax.dot_general(
+        spans = [(max(b - 1, 0) * BLOCK, min(b + 2, NT) * BLOCK) for b in range(NT)]
+        scores = [
+            lax.dot_general(
                 q_s[c, b],
                 k_s[lo:hi, :],
                 (((1,), (1,)), ((), ())),
                 preferred_element_type=jnp.float32,
             )
-            sc = sc * scale + mask[b : b + 1, lo:hi]
+            for b, (lo, hi) in enumerate(spans)
+        ]
+        outs = []
+        for b, (lo, hi) in enumerate(spans):
+            sc = scores[b] * scale + mask[b : b + 1, lo:hi]
             e = jnp.exp(sc - jnp.max(sc, axis=-1, keepdims=True))
             p = (e * (1.0 / jnp.sum(e, axis=-1, keepdims=True))).astype(jnp.bfloat16)
             o = jnp.dot(p, v_s[lo:hi, :], preferred_element_type=jnp.float32)
-            o = o.astype(jnp.bfloat16)
+            outs.append(o.astype(jnp.bfloat16))
+        for b in range(NT):
             for h in range(heads):
-                mixed[b * CR : (b + 1) * CR, h * HEAD : (h + 1) * HEAD] = o[
+                mixed[b * CR : (b + 1) * CR, h * HEAD : (h + 1) * HEAD] = outs[b][
                     h * CR : (h + 1) * CR
                 ]
 
     def project(k, c):
         width = 512
         lhs = mixed[...]
-
-        def tile(n, _):
-            at = pl.ds(pl.multiple_of(n * width, width), width)
-            part[k, c, :, at] = jnp.dot(
-                lhs, wo[:, at], preferred_element_type=jnp.float32
+        for n in range(0, dim, width):
+            part[k, c, :, n : n + width] = jnp.dot(
+                lhs, wo[:, n : n + width], preferred_element_type=jnp.float32
             ).astype(jnp.bfloat16)
-            return 0
-
-        lax.fori_loop(0, dim // width, tile, 0)
         for kind in range(4):
             rs_copy(k, c, kind).start()
 
@@ -378,16 +391,18 @@
         rs_copy(k, c, 5).start()
 
     def finish(k, c):
-        for kind in range(2, 6):
-            rs_copy(k, c, kind).wait_recv()
         f32 = jnp.float32
-        total = (
-            rows(part, k, c, t)[...].astype(f32)
-            + fl[k, c].astype(f32)
-            + fr[k, c].astype(f32)
-        )
-        y[k, c] = (x[k, c].astype(f32) + total).astype(jnp.bfloat16)
-        hop(k, c, y.at[k, c]).start()
+        for half, kinds in ((0, (3, 4)), (1, (2, 5))):
+            for kind in kinds:
+                rs_copy(k, c, kind).wait_recv()
+            at = pl.ds(half * HR, HR)
+            total = (
+                rows(part, k, c, t, half * HR, HR)[...].astype(f32)
+                + fl[k, c, at].astype(f32)
+                + fr[k, c, at].astype(f32)
+            )
+            y[k, c, at] = (x[k, c, at].astype(f32) + total).astype(jnp.bfloat16)
+            hop(k, c, half, y).start()
 
     def wait_x1(c):
         @pl.when(s == 0)
@@ -396,7 +411,13 @@
 
         @pl.when(s != 0)
         def _():
-            hop(0, c, y.at[0, c]).wait_recv()
+            for half in range(2):
+                hop(0, c, half, y).wait_recv()
+
+    def first(c):
+        wait_x1(c)
+        norm(1, c)
+        ag_start(1, c)
 
     def gather_phase(k, ahead):
         def step(c, _):
@@ -406,24 +427,30 @@
             def _():
                 if k == 1:
                     wait_x1(c + ahead)
-                ag_issue(k, c + ahead)
+                    norm(k, c + ahead)
+                ag_start(k, c + ahead)
 
             @pl.when(c >= 1)
             def _():
                 wait_opp(k, c - 1)
-                qkv(k, c - 1)
+                keys_values(k, c - 1)
+                queries(k, c - 1)
 
             return 0
 
         lax.fori_loop(0, NC, step, 0)
         wait_opp(k, NC - 1)
-        qkv(k, NC - 1)
+        keys_values(k, NC - 1)
 
     def reduce_phase(k):
         def step(c, _):
             attention(c)
             project(k, c)
 
+            @pl.when(c == 0)
+            def _():
+                queries(k, NC - 1)
+
             @pl.when(c >= 1)
             def _():
                 add_on(k, c - 1)
@@ -435,14 +462,12 @@
             return 0
 
         lax.fori_loop(0, NC, step, 0)
+        if k == 0:
+            first(0)
         add_on(k, NC - 1)
-        if k == 0:
-            wait_x1(0)
-            ag_issue(1, 0)
         finish(k, NC - 2)
         if k == 0:
-            wait_x1(1)
-            ag_issue(1, 1)
+            first(1)
         finish(k, NC - 1)
 
     def wait_tokens():
@@ -452,11 +477,8 @@
 
     @pl.when(active)
     def _():
-        for c in range(2):
-            x_load(c).wait()
-            ag_issue(0, c)
-        for c in range(2, NC):
-            x_load(c).wait()
+        ag_start(0, 0)
+        ag_start(0, 1)
         setup(0)
         for load in loads[:3]:
             load.wait()
@@ -481,11 +503,11 @@
     @pl.when(jnp.logical_not(active))
     def _():
         for c in range(NC):
-            x_load(c).wait()
 
             @pl.when(s != last)
             def _():
-                hop(0, c, x.at[0, c]).start()
+                for half in range(2):
+                    hop(0, c, half, x).start()
 
         for slot, root in ((0, last), (1, last - 1)):
 
@@ -494,11 +516,13 @@
                 pool_root(slot)
 
         for c in range(NC):
-            hop(0, c, x.at[0, c]).wait_recv()
+            for half in range(2):
+                hop(0, c, half, x).wait_recv()
 
             @pl.when(s != last)
             def _():
-                hop(1, c, x.at[1, c]).start()
+                for half in range(2):
+                    hop(1, c, half, x).start()
 
         wait_tokens()
 
@@ -535,12 +559,14 @@
         tok_copy.wait_send()
         for k in range(2):
             for c in range(NC):
-                hop(k, c, y.at[k, c]).wait_send()
+                for half in range(2):
+                    hop(k, c, half, y).wait_send()
 
     @pl.when(s != 0)
     def _():
         for c in range(NC):
-            hop(1, c, y.at[1, c]).wait_recv()
+            for half in range(2):
+                hop(1, c, half, y).wait_recv()
 
     @pl.when(s == 0)
     def _():
@@ -619,8 +645,8 @@
                 dma((2, NC, 4)),
                 dma((2, NC, 6)),
                 dma((2, NC, 6)),
-                dma((2, NC)),
-                dma((2, NC)),
+                dma((2, NC, 2)),
+                dma((2, NC, 2)),
                 dma,
                 dma,
                 dma((NT - 1,)),

time: 151 us -> 143 us (0.947)
  Pallas kernels: 146 us -> 138 us
    pallas_call x1, Pallas kernels: 146 us -> 138 us  [local(): pl.pallas_call(body, out_shape=(jax.ShapeDtypeStruct(flight_state.shape,...]
where the time goes in v2:
time: 143 us
  Pallas kernels  138 us (97%)
  local copies, waits for them, and re-layouts  3.71 us (3%)
    pallas_call x1, Pallas kernels, local(): pl.pallas_call(body, out_shape=(jax.ShapeDtypeStruct(flight_state.shape,...  138 us
    unnamed x2, local copies, waits for them, and re-layouts  3.71 us

profile of v2, /device:TPU:32, one launch (start us, length us, event | category | flops | bytes accessed | tf_op | source)
XLA Modules:
  0.0 142.6 jit_solution(12006276446394187988)
XLA Ops:
  0.6 138.3 %shard_map.167 = (bf16[1,128,3584]{2,1,0:T(8,128)(2,1)}, f32[8,3584]{1,0:T(8,128)}) custom-call(bf16[1,128,3584]{2,1,0:T(8,128)(2,1)} %refs_0_.1, s32[1,3]{1,0:T(1,128)} %refs_1_.1, s32[1,3]{1,0:T(1,128)} %refs_2_.1, bf16[2,128,3584]{2,1,0:T(8,128)(2,1)} %refs_3_.1, s32[2,3]{1,0:T(2,128)} %refs_4_.1, f32[1,3584]{1,0:T(1,128)} %refs_5_.1, ...), custom_call_target="tpu_custom_call" | custom-call | tf_op jit(solution)/shard_map/pallas_call | solution.py:610
  138.9 2.2 %copy.20 = bf16[1,128,3584]{2,1,0:T(8,128)(2,1)} copy(bf16[1,128,3584]{2,1,0:T(8,128)(2,1)} %get-tuple-element.4) | data formatting | bytes 1835008
  141.1 1.6 %copy.21 = f32[8,3584]{1,0:T(8,128)} copy(f32[8,3584]{1,0:T(8,128)} %get-tuple-element.5) | data formatting | bytes 229376

commit v3 on v2

--- a/solution.py
+++ b/solution.py
@@ -51,8 +51,8 @@
     vb,
     wo_hbm,
     list_rows,
-    cos_tab,
-    sin_tab,
+    cos_hbm,
+    sin_hbm,
     out,
     sums,
     w,
@@ -90,6 +90,11 @@
     pp_r,
     pb_s,
     pb_r,
+    sum_buf,
+    sum_sem,
+    cos_tab,
+    sin_tab,
+    tab_sem,
 ):
     s = lax.axis_index("section")
     t = lax.axis_index("tensor")
@@ -116,6 +121,11 @@
         pltpu.make_async_copy(wo_hbm.at[0], wo, w_sem.at[3]),
     ]
 
+    tables = [
+        pltpu.make_async_copy(cos_hbm, cos_tab, tab_sem.at[0]),
+        pltpu.make_async_copy(sin_hbm, sin_tab, tab_sem.at[1]),
+    ]
+
     def x_load(c):
         return pltpu.make_async_copy(
             flight.at[0, pl.ds(c * CR, CR)], x.at[0, c], x_sem.at[c]
@@ -133,7 +143,7 @@
 
     @pl.when(active)
     def _():
-        for load in loads:
+        for load in tables + loads:
             load.start()
 
     @pl.when(s == 0)
@@ -291,15 +301,15 @@
         for b in range(NT):
             for kb_ in range(NT):
                 ok = (info[b][0] == info[kb_][0]) & (i + BLOCK * info[kb_][1] < info[kb_][2])
-                mask[b : b + 1, kb_ * BLOCK : (kb_ + 1) * BLOCK] = jnp.where(ok, 0.0, NEG)
+                mask[k, b : b + 1, kb_ * BLOCK : (kb_ + 1) * BLOCK] = jnp.where(ok, 0.0, NEG)
         for b in range(NT):
             second = info[b][1] > 0
             for c in range(NC):
                 lo, hi = c * CR, (c + 1) * CR
-                rc[c, b * CR : (b + 1) * CR] = jnp.where(
+                rc[k, c, b * CR : (b + 1) * CR] = jnp.where(
                     second, cos_tab[BLOCK + lo : BLOCK + hi], cos_tab[lo:hi]
                 )
-                rs[c, b * CR : (b + 1) * CR] = jnp.where(
+                rs[k, c, b * CR : (b + 1) * CR] = jnp.where(
                     second, sin_tab[BLOCK + lo : BLOCK + hi], sin_tab[lo:hi]
                 )
 
@@ -317,12 +327,12 @@
         ag_recv(k, c, 2).wait_recv()
         ag_recv(k, c, 3).wait_recv()
 
-    def rope(v, c):
-        return (v * rc[c] + pltpu.roll(v, HEAD // 2, 1) * rs[c]).astype(jnp.bfloat16)
+    def rope(v, k, c):
+        return (v * rc[k, c] + pltpu.roll(v, HEAD // 2, 1) * rs[k, c]).astype(jnp.bfloat16)
 
     def keys_values(k, c):
         kv = jnp.dot(g[k, c], w[:, 0 : 2 * HEAD], preferred_element_type=jnp.float32)
-        key = rope(kv[:, :HEAD] + kb[...], c)
+        key = rope(kv[:, :HEAD] + kb[...], k, c)
         val = (kv[:, HEAD:] + vb[...]).astype(jnp.bfloat16)
         for b in range(NT):
             at = pl.ds(pl.multiple_of(b * BLOCK + c * CR, CR), CR)
@@ -341,11 +351,11 @@
             for j in range(n):
                 h = h0 + j
                 v = q[:, j * HEAD : (j + 1) * HEAD] + qb[:, h * HEAD : (h + 1) * HEAD]
-                v = rope(v, c)
+                v = rope(v, k, c)
                 for b in range(NT):
                     q_s[c, b, h * CR : (h + 1) * CR, :] = v[b * CR : (b + 1) * CR]
 
-    def attention(c):
+    def attention(k, c):
         scale = 1.0 / math.sqrt(HEAD)
         spans = [(max(b - 1, 0) * BLOCK, min(b + 2, NT) * BLOCK) for b in range(NT)]
         scores = [
@@ -359,7 +369,7 @@
         ]
         outs = []
         for b, (lo, hi) in enumerate(spans):
-            sc = scores[b] * scale + mask[b : b + 1, lo:hi]
+            sc = scores[b] * scale + mask[k, b : b + 1, lo:hi]
             e = jnp.exp(sc - jnp.max(sc, axis=-1, keepdims=True))
             p = (e * (1.0 / jnp.sum(e, axis=-1, keepdims=True))).astype(jnp.bfloat16)
             o = jnp.dot(p, v_s[lo:hi, :], preferred_element_type=jnp.float32)
@@ -419,6 +429,31 @@
         norm(1, c)
         ag_start(1, c)
 
+    sums_copy = pltpu.make_async_copy(sum_buf, sums, sum_sem)
+
+    def sum_lists():
+        for slot, root in ((0, last), (1, last - 1)):
+
+            @pl.when(s != root)
+            def _():
+                pool_bcast(slot, 0).wait_recv()
+
+        own = sum_buf.shape[0]
+        mine = ((s * NT + t) * own + lax.broadcasted_iota(jnp.int32, (own, HEAD), 0)).astype(jnp.float32)
+        total = jnp.zeros((own, dim), jnp.float32)
+        for slot in range(2):
+            for p in range(3):
+                hit = mine == pool[slot, p : p + 1, dim : dim + HEAD]
+                hit = jnp.where(hit, 1.0, 0.0)[:, :1]
+                total = total + hit * pool[slot, p : p + 1, 0:dim]
+        sum_buf[...] = total
+        sums_copy.start()
+
+    def wait_tokens():
+        @pl.when(s != 0)
+        def _():
+            tok_copy.wait_recv()
+
     def gather_phase(k, ahead):
         def step(c, _):
             forward(k, c)
@@ -436,6 +471,13 @@
                 keys_values(k, c - 1)
                 queries(k, c - 1)
 
+            if k == 0:
+
+                @pl.when(c == 1)
+                def _():
+                    wait_tokens()
+                    setup(1)
+
             return 0
 
         lax.fori_loop(0, NC, step, 0)
@@ -444,7 +486,7 @@
 
     def reduce_phase(k):
         def step(c, _):
-            attention(c)
+            attention(k, c)
             project(k, c)
 
             @pl.when(c == 0)
@@ -470,23 +512,19 @@
             first(1)
         finish(k, NC - 1)
 
-    def wait_tokens():
-        @pl.when(s != 0)
-        def _():
-            tok_copy.wait_recv()
-
     @pl.when(active)
     def _():
         ag_start(0, 0)
         ag_start(0, 1)
+        for load in tables:
+            load.wait()
         setup(0)
         for load in loads[:3]:
             load.wait()
         gather_phase(0, 2)
         loads[3].wait()
         reduce_phase(0)
-        wait_tokens()
-        setup(1)
+        sum_lists()
         gather_phase(1, 2)
         reduce_phase(1)
 
@@ -525,6 +563,7 @@
                     hop(1, c, half, x).start()
 
         wait_tokens()
+        sum_lists()
 
         for slot, root in ((0, last), (1, last - 1)):
 
@@ -538,21 +577,7 @@
                 for d in range(1, NT):
                     pool_parts(d).wait_send()
 
-    for slot, root in ((0, last), (1, last - 1)):
-
-        @pl.when(s != root)
-        def _():
-            pool_bcast(slot, 0).wait_recv()
-
-    own = sums.shape[0]
-    mine = ((s * NT + t) * own + lax.broadcasted_iota(jnp.int32, (own, HEAD), 0)).astype(jnp.float32)
-    total = jnp.zeros((own, dim), jnp.float32)
-    for slot in range(2):
-        for p in range(3):
-            hit = mine == pool[slot, p : p + 1, dim : dim + HEAD]
-            hit = jnp.where(hit, 1.0, 0.0)[:, :1]
-            total = total + hit * pool[slot, p : p + 1, 0:dim]
-    sums[...] = total
+    sums_copy.wait()
 
     @pl.when(s != last)
     def _():
@@ -607,16 +632,16 @@
         def body(*refs):
             kernel(n_sections, n_layers, *refs)
 
-        return pl.pallas_call(
+        state, sums = pl.pallas_call(
             body,
             out_shape=(
                 jax.ShapeDtypeStruct(flight_state.shape, bf16),
                 jax.ShapeDtypeStruct((own, dim), f32),
             ),
             in_specs=[
-                hbm, smem, smem, hbm, smem, vmem, hbm, vmem, hbm, vmem, hbm, vmem, hbm, smem, vmem, vmem,
+                hbm, smem, smem, hbm, smem, vmem, hbm, vmem, hbm, vmem, hbm, vmem, hbm, smem, hbm, hbm,
             ],
-            out_specs=(hbm, vmem),
+            out_specs=(hbm, hbm),
             scratch_shapes=[
                 pltpu.VMEM((dim, qcols + 2 * HEAD), bf16),
                 pltpu.VMEM((qcols, dim), bf16),
@@ -632,9 +657,9 @@
                 pltpu.VMEM((NT * BLOCK, HEAD), bf16),
                 pltpu.VMEM((NT * BLOCK, HEAD), bf16),
                 pltpu.VMEM((NT * CR, qcols), bf16),
-                pltpu.VMEM((NC, NT * CR, HEAD), f32),
-                pltpu.VMEM((NC, NT * CR, HEAD), f32),
-                pltpu.VMEM((8, NT * BLOCK), f32),
+                pltpu.VMEM((2, NC, NT * CR, HEAD), f32),
+                pltpu.VMEM((2, NC, NT * CR, HEAD), f32),
+                pltpu.VMEM((2, 8, NT * BLOCK), f32),
                 pltpu.VMEM((2, 8, HEAD), jnp.int32),
                 pltpu.VMEM((2, 8, dim + HEAD), f32),
                 pltpu.VMEM((NT, 8, dim), f32),
@@ -652,6 +677,11 @@
                 dma((NT - 1,)),
                 dma((NT - 1,)),
                 dma((n_sections,)),
+                dma((2,)),
+                pltpu.VMEM((own, dim), f32),
+                dma,
+                pltpu.VMEM((2 * BLOCK, HEAD), f32),
+                pltpu.VMEM((2 * BLOCK, HEAD), f32),
                 dma((2,)),
             ],
             compiler_params=pltpu.CompilerParams(
@@ -678,6 +708,24 @@
             jnp.asarray(sin_np),
         )
 
+        def write(state_in, sums_in, state_out, sums_out):
+            state_out[...] = state_in[...]
+            sums_out[...] = sums_in[...]
+
+        steps = 2
+        one = pl.BlockSpec((1, BLOCK // steps, dim), lambda i: (0, i, 0))
+        two = pl.BlockSpec((own, dim), lambda i: (0, 0))
+        return pl.pallas_call(
+            write,
+            grid=(steps,),
+            out_shape=(
+                jax.ShapeDtypeStruct(flight_state.shape, bf16),
+                jax.ShapeDtypeStruct((own, dim), f32),
+            ),
+            in_specs=[one, two],
+            out_specs=(one, two),
+        )(state, sums)
+
     in_specs = (
         P("section", "tensor", None),
         P("section", None),

time: 143 us -> 140 us (0.979)
  local copies, waits for them, and re-layouts: 3.71 us -> 0 us
  Pallas kernels: 138 us -> 140 us
    unnamed x2 -> x0, local copies, waits for them, and re-layouts: 3.71 us -> none
    pallas_call x0 -> x1, Pallas kernels: none -> 2.06 us  [local(): pl.pallas_call(write, grid=(steps,), out_shape=(jax.ShapeDtypeStruct(flig...]
where the time goes in v3:
time: 140 us
  Pallas kernels  140 us (100%)
    pallas_call x1, Pallas kernels, local(): pl.pallas_call(body, out_shape=(jax.ShapeDtypeStruct(flight_state.shape,...  138 us

profile of v3, /device:TPU:32, one launch (start us, length us, event | category | flops | bytes accessed | tf_op | source)
XLA Modules:
  0.0 140.2 jit_solution(15189827774393337761)
XLA Ops:
  0.6 137.5 %shard_map.167 = (bf16[1,128,3584]{2,1,0:T(8,128)(2,1)}, f32[8,3584]{1,0:T(8,128)}) custom-call(bf16[1,128,3584]{2,1,0:T(8,128)(2,1)} %refs_0_.1, s32[1,3]{1,0:T(1,128)} %refs_1_.1, s32[1,3]{1,0:T(1,128)} %refs_2_.1, bf16[2,128,3584]{2,1,0:T(8,128)(2,1)} %refs_3_.1, s32[2,3]{1,0:T(2,128)} %refs_4_.1, f32[1,3584]{1,0:T(1,128)} %refs_5_.1, ...), custom_call_target="tpu_custom_call" | custom-call | tf_op jit(solution)/shard_map/pallas_call | solution.py:635
  138.2 2.1 %shard_map.168 = (bf16[1,128,3584]{2,1,0:T(8,128)(2,1)}, f32[8,3584]{1,0:T(8,128)}) custom-call(bf16[1,128,3584]{2,1,0:T(8,128)(2,1)} %get-tuple-element.4.state_in, f32[8,3584]{1,0:T(8,128)} %get-tuple-element.5.sums_in), custom_call_target="tpu_custom_call" | custom-call | tf_op jit(solution)/shard_map/pallas_call | solution.py:718

commit v4 on v3

--- a/solution.py
+++ b/solution.py
@@ -497,6 +497,12 @@
             def _():
                 add_on(k, c - 1)
 
+            if k == 0:
+
+                @pl.when(c == NC - 1)
+                def _():
+                    first(0)
+
             @pl.when(c >= 2)
             def _():
                 finish(k, c - 2)
@@ -504,8 +510,6 @@
             return 0
 
         lax.fori_loop(0, NC, step, 0)
-        if k == 0:
-            first(0)
         add_on(k, NC - 1)
         finish(k, NC - 2)
         if k == 0:

time: 140 us -> 140 us (level)
  no operation moved by 1% of the time
where the time goes in v4:
time: 140 us
  Pallas kernels  140 us (100%)
    pallas_call x1, Pallas kernels, local(): pl.pallas_call(body, out_shape=(jax.ShapeDtypeStruct(flight_state.shape,...  138 us

profile of v4, /device:TPU:32, one launch (start us, length us, event | category | flops | bytes accessed | tf_op | source)
XLA Modules:
  0.0 140.2 jit_solution(17460395848271994353)
XLA Ops:
  0.6 137.5 %shard_map.167 = (bf16[1,128,3584]{2,1,0:T(8,128)(2,1)}, f32[8,3584]{1,0:T(8,128)}) custom-call(bf16[1,128,3584]{2,1,0:T(8,128)(2,1)} %refs_0_.1, s32[1,3]{1,0:T(1,128)} %refs_1_.1, s32[1,3]{1,0:T(1,128)} %refs_2_.1, bf16[2,128,3584]{2,1,0:T(8,128)(2,1)} %refs_3_.1, s32[2,3]{1,0:T(2,128)} %refs_4_.1, f32[1,3584]{1,0:T(1,128)} %refs_5_.1, ...), custom_call_target="tpu_custom_call" | custom-call | tf_op jit(solution)/shard_map/pallas_call | solution.py:639
  138.2 2.1 %shard_map.168 = (bf16[1,128,3584]{2,1,0:T(8,128)(2,1)}, f32[8,3584]{1,0:T(8,128)}) custom-call(bf16[1,128,3584]{2,1,0:T(8,128)(2,1)} %get-tuple-element.4.state_in, f32[8,3584]{1,0:T(8,128)} %get-tuple-element.5.sums_in), custom_call_target="tpu_custom_call" | custom-call | tf_op jit(solution)/shard_map/pallas_call | solution.py:722
